TPU v7x, 32 devices: a whole 2x2x4 slice. The times are simulated.
32 devices in a mesh: rows: 32 (over z, y, x, core).
Axes of the slice: x: 2, y: 2, z: 4, core: 2. Of those that a mesh axis runs over, the one named last changes fastest.
Arguments:
- trailing: float32 [16384, 1024], P('rows'), may hold values from -50 to 50
- leaf_vectors: float32 [16384, 256], P('rows'), may hold values from -2 to 2, as said below
- leaf_factors: float32 [8192, 256], P('rows'), may hold values from -2 to 2, as said below
- tree_vectors: float32 [8192, 256], P('rows'), may hold values from -2 to 2, as said below
- tree_factors: float32 [8192, 256], P('rows'), may hold values from -2 to 2, as said below
- inverse_factor: float32 [256, 256], replicated, may hold values from -2 to 2, as said below
Outputs:
- updated: float32 [16384, 1024], P('rows')
- panel_basis: float32 [16384, 256], P('rows')
- panel_gram: float32 [256, 256], replicated
Inputs may be any that keep to these rules, and one draw needn't show every extreme that they name: Within each leaf, rows 0 to 255 of leaf_vectors form a unit lower triangular matrix (ones on the diagonal, zeros above); leaf_factors_p is the upper triangular factor for which I - leaf_vectors_p leaf_factors_p leaf_vectors_p^T is orthogonal. `leaf_factors`: each block is upper triangular and is the factor described for leaf_vectors. `tree_vectors`: each block is upper triangular, diagonal included; with Y = [I; tree_vectors_q], I - Y tree_factors_q Y^T is orthogonal. `tree_factors`: each block is upper triangular and is the factor described for tree_vectors. `inverse_factor`: upper triangular with a positive diagonal.
All inputs are finite; a program needn't handle non-finite values.
Results may differ from a plain program's by a relative error of at most 0.00018.
Values sent between devices are 32-bit elements; how exact they have to be, the bound alone decides.
No kernel may reach another device: no remote copies, remote signals or barrier semaphores. Data moves between devices by JAX's collectives and lax.ppermute only.
A program may use at most 64 MiB of HBM per device.

v0:
```python
import functools
import jax
import jax.numpy as jnp
from jax import lax
from jax.experimental import pallas as pl
from jax.experimental.pallas import tpu as pltpu
from jax.sharding import PartitionSpec as P

F32 = jnp.float32
BF16 = jnp.bfloat16
EXTRA = 8
PARAMS = pltpu.CompilerParams(vmem_limit_bytes=40 * 1024 * 1024)
WHOLE = pl.BlockSpec(memory_space=pltpu.VMEM)
SCALAR = pl.BlockSpec(memory_space=pltpu.SMEM)


def halves(value):
    high = value.astype(BF16)
    return high, (value - high.astype(F32)).astype(BF16)


def times(left, right, sides):
    dims = ((sides[:1], sides[1:]), ((), ()))
    dot = functools.partial(lax.dot_general, dimension_numbers=dims, preferred_element_type=F32)
    return dot(left[0], right[0]) + (dot(left[0], right[1]) + dot(left[1], right[0]))


def plain(left, right):
    return times(left, right, (1, 0))


def by_transpose(left, right):
    return times(left, right, (1, 1))


def pack_kernel(vectors_ref, factors_ref, out_ref):
    width = vectors_ref.shape[0]
    row = lax.broadcasted_iota(jnp.int32, (width, width), 0)
    col = lax.broadcasted_iota(jnp.int32, (width, width), 1)
    factors = factors_ref[...]
    out_ref[:width] = jnp.where(row > col, factors.T, vectors_ref[...])
    diagonal = jnp.sum(jnp.where(row == col, factors, 0.0), axis=0, keepdims=True)
    out_ref[width:] = jnp.broadcast_to(diagonal, (EXTRA, width))


def unpack(value):
    width = value.shape[1]
    packed = value[:width]
    row = lax.broadcasted_iota(jnp.int32, (width, width), 0)
    col = lax.broadcasted_iota(jnp.int32, (width, width), 1)
    diagonal = jnp.broadcast_to(value[width : width + 1], (width, width))
    vectors = jnp.where(row <= col, packed, 0.0)
    factors = jnp.where(row > col, packed, jnp.where(row == col, diagonal, 0.0))
    return halves(vectors), halves(factors)


def place(me):
    return (me >> 1) & 3


def by_place(me, parts, wanted):
    source = place(me) ^ wanted
    out = parts[0]
    for r in range(1, 4):
        out = jnp.where(source == r, parts[r], out)
    return out


def tree_node(low, high, reflector):
    vectors, factors = reflector
    node = by_transpose(halves(low + plain(halves(high), vectors)), factors)
    return low - node, high - by_transpose(halves(node), vectors)


def leaf_kernel(
    me_ref, trailing_ref, vectors_ref, factors_ref, inverse_ref,
    own_ref, away_ref, updated_ref, basis_ref, head_ref, gram_ref, v_high, v_low, f_high, f_low,
):
    block = pl.program_id(0)
    width = factors_ref.shape[0]
    half = width // 2
    core = me_ref[0] % 2
    mine = pl.multiple_of(core * half, half)
    other = pl.multiple_of((1 - core) * half, half)

    @pl.when(block == 0)
    def _():
        v_high[...], v_low[...] = halves(vectors_ref[...])
        f_high[...], f_low[...] = halves(factors_ref[...])

    vectors = (v_high[...], v_low[...])
    part = trailing_ref[...].T
    split = halves(part)
    coeffs = plain(halves(plain(split, vectors)), (f_high[...], f_low[...]))
    out = part - by_transpose(halves(coeffs), vectors)
    head_ref[...] = out[:, :width]
    rows = pl.ds(pl.multiple_of(block * half, half), half)
    own_ref[rows] = head_ref[pl.ds(mine, half)]
    away_ref[rows] = head_ref[pl.ds(other, half)]
    rest = out[:, width:].T
    updated_ref[...] = rest

    @pl.when(block == 0)
    def _():
        gram_ref[...] = by_transpose(split, split)
        last = pl.ds(own_ref.shape[0] - half, half)
        own_ref[last] = gram_ref[pl.ds(mine, half)]
        away_ref[last] = gram_ref[pl.ds(other, half)]
        basis_ref[...] = plain(halves(rest), halves(inverse_ref[...]))


def core_kernel(
    me_ref, own_ref, there_ref, packed_ref, *refs
):
    sends, dones, (low_ref, high_ref) = refs[:4], refs[4:8], refs[8:]
    me = me_ref[0]
    width = own_ref.shape[1]
    half = width // 2
    quarter = half // 4
    count = own_ref.shape[0] // half - 1
    odd = me % 2 == 1
    mine, there = own_ref[: count * half], there_ref[: count * half]
    low = jnp.where(odd, there, mine)
    high = jnp.where(odd, mine, there)
    low, high = tree_node(low, high, unpack(packed_ref[...]))
    low_ref[: count * half] = low
    low_ref[count * half :] = own_ref[count * half :] + there_ref[count * half :]
    high_ref[...] = high
    for r in range(4):
        start = (place(me) ^ r) * quarter
        for b in range(count + 1):
            source = pl.ds(pl.multiple_of(b * half + start, quarter), quarter)
            target = slice(b * quarter, (b + 1) * quarter)
            sends[r][target] = low_ref[source]
            if b < count:
                dones[r][target] = high_ref[source]


def plane_kernel(me_ref, *refs, level):
    gots, packeds, (head_ref, send_ref, done_ref) = refs[:4], refs[4:8], refs[8:]
    me = me_ref[0]
    cols = done_ref.shape[1]
    parts = [ref[...] for ref in packeds]
    reflectors = [unpack(by_place(me, parts, j)) for j in range(4)]
    parts = [ref[:cols] for ref in gots]
    heads = [by_place(me, parts, j) for j in range(4)]
    gram = gots[0][cols:] + gots[1][cols:] + (gots[2][cols:] + gots[3][cols:])
    heads[0], heads[1] = tree_node(heads[0], heads[1], reflectors[1])
    heads[2], heads[3] = tree_node(heads[2], heads[3], reflectors[3])
    heads[0], heads[2] = tree_node(heads[0], heads[2], reflectors[2])
    for j in range(4):
        done_ref[j] = heads[j]
    head_ref[...] = heads[0]
    upper = (me >> level) % 2 == 1
    send_ref[:cols] = jnp.where(upper, plain(halves(heads[0]), reflectors[0][0]), heads[0])
    send_ref[cols:] = gram


def line_kernel(
    me_ref, head_ref, result_ref, mine_ref, there_ref, held_ref, node_ref, next_ref,
    head_out, result_out, send_ref, *, level,
):
    me = me_ref[0]
    cols = head_ref.shape[0]
    low, result, gram = line_node(
        me, head_ref, result_ref, mine_ref, there_ref, held_ref, node_ref, level
    )
    ahead = (me >> (level + 1)) % 2 == 1
    following = unpack(next_ref[...])
    head_out[...] = low
    result_out[...] = result
    send_ref[:cols] = jnp.where(ahead, plain(halves(low), following[0]), low)
    send_ref[cols:] = gram


def line_node(me, head_ref, result_ref, mine_ref, there_ref, held_ref, node_ref, level):
    cols = head_ref.shape[0]
    upper = (me >> level) % 2 == 1
    held = unpack(held_ref[...])
    node = unpack(node_ref[...])
    head = head_ref[...]
    there = there_ref[:cols]
    coeffs = by_transpose(halves(mine_ref[:cols] + there), node[1])
    low = jnp.where(upper, there, head) - coeffs
    plane = me >> 3
    below = (1 << (level - 2)) - 1
    second = (plane & below) == (1 << (level - 3))
    result = jnp.where(second, head - by_transpose(halves(coeffs), held[0]), result_ref[...])
    return low, result, mine_ref[cols:] + there_ref[cols:]


def last_kernel(
    me_ref, head_ref, result_ref, mine_ref, there_ref, held_ref, node_ref, done_ref, *refs, level
):
    sends, all_ref = refs[:4], refs[4]
    me = me_ref[0]
    cols = head_ref.shape[0]
    low, result, gram = line_node(
        me, head_ref, result_ref, mine_ref, there_ref, held_ref, node_ref, level
    )
    all_ref[0] = jnp.where((me >> 3) == 0, low, result)
    for j in range(1, 4):
        all_ref[j] = done_ref[j]
    quarter = gram.shape[0]
    for r in range(4):
        sends[r][:cols] = all_ref[place(me) ^ r]
        sends[r][cols : cols + quarter] = low[:quarter]
        sends[r][cols + quarter :] = gram


def pass_kernel(me_ref, *refs):
    backs, dones, out_ref = refs[:4], refs[4:8], refs[8]
    odd = me_ref[0] % 2 == 1
    cols = dones[0].shape[0]
    for r in range(4):
        out_ref[r, :cols] = jnp.where(odd, backs[r][:cols], dones[r][...])
        out_ref[r, cols:] = backs[r][cols:]


def final_kernel(me_ref, *refs, total):
    backs, dones = refs[:4], refs[4:8]
    there_ref, inverse_ref, _, _, updated_ref, basis_ref, gram_ref = refs[8:15]
    head_ref, panel_ref, sum_ref = refs[15:]
    block = pl.program_id(0)
    width = inverse_ref.shape[0]
    half = width // 2
    quarter = half // 4
    cols = dones[0].shape[0]
    me = me_ref[0]
    core = me % 2
    odd = core == 1
    rows = pl.ds(pl.multiple_of(block * quarter, quarter), quarter)

    def target(part, r):
        return pl.ds(pl.multiple_of(part * half + (place(me) ^ r) * quarter, quarter), quarter)

    for r in range(4):
        there = there_ref[r, rows]
        head_ref[target(0, r)] = jnp.where(odd, there, backs[r][rows])
        head_ref[target(1, r)] = jnp.where(odd, dones[r][rows], there)
    head = head_ref[...].T
    updated_ref[...] = head

    @pl.when(block == 0)
    def _():
        basis = plain(halves(head), halves(inverse_ref[...]))
        basis_ref[...] = jnp.where(me == 0, 0.0, basis)
        for r in range(4):
            panel_ref[target(core, r)] = backs[r][cols : cols + quarter]
            sum_ref[target(core, r)] = backs[r][cols + quarter :]
            panel_ref[target(1 - core, r)] = there_ref[r, cols : cols + quarter]
            sum_ref[target(1 - core, r)] = there_ref[r, cols + quarter :]
        panel = halves(panel_ref[...])
        gram_ref[...] = (sum_ref[...] - by_transpose(panel, panel)) / total


def body(trailing, leaf_vectors, leaf_factors, tree_vectors, tree_factors, inverse_factor):
    rows, columns = trailing.shape
    width = leaf_vectors.shape[1]
    half = width // 2
    quarter = half // 4
    count = columns // width
    cols = count * quarter
    devices = lax.axis_size("rows")
    levels = devices.bit_length() - 1
    me = lax.axis_index("rows").astype(jnp.int32)
    me_array = me.reshape(1)
    odd = me % 2 == 1

    def exchange(value, shift, member=lambda i: True):
        pairs = [(i, i ^ shift) for i in range(devices) if member(i)]
        return lax.ppermute(value, "rows", pairs)

    def even(i):
        return i % 2 == 0

    def both(value):
        return jnp.where(odd, exchange(value, 1, even), value)

    def shape(*dims):
        return jax.ShapeDtypeStruct(dims, F32)

    def whole_call(kernel, operands, outs, scratch=()):
        return pl.pallas_call(
            kernel,
            out_shape=outs,
            in_specs=[SCALAR] + [WHOLE] * len(operands),
            out_specs=tuple(WHOLE for _ in outs),
            scratch_shapes=[pltpu.VMEM(dims, F32) for dims in scratch],
            compiler_params=PARAMS,
        )(me_array, *operands)

    packed = pl.pallas_call(
        pack_kernel,
        out_shape=shape(width + EXTRA, width),
        in_specs=[WHOLE] * 2,
        out_specs=WHOLE,
        compiler_params=PARAMS,
    )(tree_vectors, tree_factors)
    plane_even = [exchange(packed, 2 * r, even) for r in range(1, 4)]
    packed_there = exchange(packed, 1)
    chip_low = jnp.where(odd, packed_there, packed)
    chip_high = jnp.where(odd, packed, packed_there)

    leaf_rows = count * half + half
    own, away, updated, basis = pl.pallas_call(
        leaf_kernel,
        grid=(count,),
        out_shape=(shape(leaf_rows, width), shape(leaf_rows, width), shape(rows, columns), shape(rows, width)),
        in_specs=[
            SCALAR,
            pl.BlockSpec((rows, width), lambda b: (0, b)),
            pl.BlockSpec((rows, width), lambda b: (0, 0)),
            pl.BlockSpec((width, width), lambda b: (0, 0)),
            pl.BlockSpec((width, width), lambda b: (0, 0)),
        ],
        out_specs=(
            pl.BlockSpec((leaf_rows, width), lambda b: (0, 0)),
            pl.BlockSpec((leaf_rows, width), lambda b: (0, 0)),
            pl.BlockSpec((width, width), lambda b: (1, b)),
            pl.BlockSpec((width, width), lambda b: (1, 0)),
        ),
        scratch_shapes=[
            pltpu.VMEM((width, width), F32),
            pltpu.VMEM((width, width), F32),
            pltpu.VMEM((rows, width), BF16),
            pltpu.VMEM((rows, width), BF16),
            pltpu.VMEM((width, width), BF16),
            pltpu.VMEM((width, width), BF16),
        ],
        compiler_params=PARAMS,
    )(me_array, trailing, leaf_vectors, leaf_factors, inverse_factor)
    away = exchange(away, 1)

    outs = whole_call(
        core_kernel, (own, away, chip_high),
        tuple([shape(cols + quarter, width)] * 4 + [shape(cols, width)] * 4),
        ((leaf_rows, width), (count * half, width)),
    )
    sends, dones = outs[:4], outs[4:]
    gots = [sends[0]] + [exchange(sends[r], 2 * r) for r in range(1, 4)]

    plane_parts = [chip_low] + [both(part) for part in plane_even]
    held = by_place(me, plane_parts, 0)
    head, send, plane_done = whole_call(
        functools.partial(plane_kernel, level=3), (*gots, *plane_parts),
        (shape(cols, width), shape(cols + quarter, width), shape(4, cols, width)),
    )

    result = head
    for level in range(3, levels):
        up = (me >> level) % 2 == 1
        last = level == levels - 1
        if last:
            other = both(exchange(held, 1 << level, lambda i: even(i) and (i >> level) % 2 == 1))
        else:
            other = both(exchange(held, 1 << level, even))
        node = jnp.where(up, held, other)
        there = exchange(send, 1 << level)
        operands = (head, result, send, there, held, node)
        if last:
            sends = whole_call(
                functools.partial(last_kernel, level=level), (*operands, plane_done),
                tuple([shape(cols + 2 * quarter, width)] * 4), ((4, cols, width),),
            )
        else:
            held = jnp.where(up, other, held)
            head, result, send = whole_call(
                functools.partial(line_kernel, level=level), (*operands, held),
                (shape(cols, width), shape(cols, width), shape(cols + quarter, width)),
            )

    backs = [sends[0]] + [exchange(sends[r], 2 * r) for r in range(1, 4)]
    (back,) = whole_call(pass_kernel, (*backs, *dones), (shape(4, cols + 2 * quarter, width),))
    there = exchange(back, 1)

    def fixed(*dims):
        return pl.BlockSpec(dims, lambda b: (0,) * len(dims))

    return pl.pallas_call(
        functools.partial(final_kernel, total=float(rows * devices)),
        grid=(count,),
        out_shape=(shape(rows, columns), shape(rows, width), shape(width, width)),
        in_specs=[SCALAR]
        + [fixed(cols + 2 * quarter, width)] * 4
        + [fixed(cols, width)] * 4
        + [fixed(*there.shape), fixed(width, width)]
        + [pl.BlockSpec(memory_space=pl.ANY)] * 2,
        out_specs=(pl.BlockSpec((width, width), lambda b: (0, b)), fixed(width, width), fixed(width, width)),
        scratch_shapes=[pltpu.VMEM((width, width), F32)] * 3,
        input_output_aliases={11: 0, 12: 1},
        compiler_params=PARAMS,
    )(me_array, *backs, *dones, there, inverse_factor, updated, basis)


def solution(mesh):
    in_specs = (
        P("rows", None),
        P("rows", None),
        P("rows", None),
        P("rows", None),
        P("rows", None),
        P(),
    )
    out_specs = (P("rows", None), P("rows", None), P())
    return jax.shard_map(body, mesh=mesh, in_specs=in_specs, out_specs=out_specs, check_vma=False)
```

profile of v0, /device:TPU:0, one launch (start us, length us, event | category | flops | bytes accessed | tf_op | source)
XLA Modules:
  0.0 97.9 jit_solution(18388360255241873095)
XLA Ops:
  2.7 5.0 %collective-permute-start.7 = (f32[264,256]{1,0:T(8,128)S(1)}, f32[264,256]{1,0:T(8,128)}, u32[]{:S(2)}, u32[]{:S(2)}) collective-permute-start(f32[264,256]{1,0:T(8,128)S(1)} %shard_map.86), channel_id=1, source_target_pairs={{0,4},{2,6},{4,0},{6,2},{8,12},{10,14},{12,8},{14,10},{16,20},{18,... | collective-permute-start | bytes 811016 | tf_op jit(solution)/shard_map/ppermute | solution.py:272
  7.7 3.4 %collective-permute-start.5 = (f32[264,256]{1,0:T(8,128)S(1)}, f32[264,256]{1,0:T(8,128)}, u32[]{:S(2)}, u32[]{:S(2)}) collective-permute-start(f32[264,256]{1,0:T(8,128)S(1)} %shard_map.86), channel_id=1, source_target_pairs={{0,2},{2,0},{4,6},{6,4},{8,10},{10,8},{12,14},{14,12},{16,18},{18,... | collective-permute-start | bytes 811016 | tf_op jit(solution)/shard_map/ppermute | solution.py:272
  11.1 1.9 %collective-permute-start.9 = (f32[264,256]{1,0:T(8,128)S(1)}, f32[264,256]{1,0:T(8,128)}, u32[]{:S(2)}, u32[]{:S(2)}) collective-permute-start(f32[264,256]{1,0:T(8,128)S(1)} %shard_map.86), channel_id=1, source_target_pairs={{0,6},{2,4},{4,2},{6,0},{8,14},{10,12},{12,10},{14,8},{16,22},{18,... | collective-permute-start | bytes 811016 | tf_op jit(solution)/shard_map/ppermute | solution.py:272
  13.1 2.4 %collective-permute-start.8 = (f32[264,256]{1,0:T(8,128)}, f32[264,256]{1,0:T(8,128)S(1)}, u32[]{:S(2)}, u32[]{:S(2)}) collective-permute-start(f32[264,256]{1,0:T(8,128)} %collective-permute-done.7), channel_id=1, source_target_pairs={{0,1},{2,3},{4,5},{6,7},{8,9},{10,11},{12,13},{14,15},{16,17},{18,... | collective-permute-start | bytes 811016 | tf_op jit(solution)/shard_map/ppermute | solution.py:272
  17.5 3.0 %collective-permute-done.9 = f32[264,256]{1,0:T(8,128)} collective-permute-done((f32[264,256]{1,0:T(8,128)S(1)}, f32[264,256]{1,0:T(8,128)}, u32[]{:S(2)}, u32[]{:S(2)}) %collective-permute-start.9) | collective-permute-done | bytes 270368 | tf_op jit(solution)/shard_map/ppermute | solution.py:272
  20.5 2.0 %collective-permute-start.10 = (f32[264,256]{1,0:T(8,128)}, f32[264,256]{1,0:T(8,128)}, u32[]{:S(2)}, u32[]{:S(2)}) collective-permute-start(f32[264,256]{1,0:T(8,128)} %collective-permute-done.9), channel_id=1, source_target_pairs={{0,1},{2,3},{4,5},{6,7},{8,9},{10,11},{12,13},{14,15},{16,17},{18,... | collective-permute-start | bytes 811016 | tf_op jit(solution)/shard_map/ppermute | solution.py:272
  23.9 2.1 %select_select_fusion.1 = (f32[264,256]{1,0:T(8,128)S(1)}, f32[264,256]{1,0:T(8,128)S(1)}, f32[264,256]{1,0:T(8,128)S(1)}, f32[264,256]{1,0:T(8,128)S(1)}, f32[264,256]{1,0:T(8,128)}, /*index=5*/f32[264,256]{1,0:T(8,128)}) fusion(pred[]{:T(512)S(6)} %eq.25, pred[]{:T(512)S(6)} %eq.24, pred[]{:T(512)S(6)} %eq.23, f32[264,256]{1,0:T(8,128)} %collective-permute-done.10, ...), kind=kLoop, calls=%fused_computation.1 | loop fusion | flops 540672 | bytes 3784708 | tf_op jit(solution)/shard_map/jit(_where)/select_n | solution.py:65
  26.0 3.5 %collective-permute-start.12 = (f32[264,256]{1,0:T(8,128)S(1)}, f32[264,256]{1,0:T(8,128)S(1)}, u32[]{:S(2)}, u32[]{:S(2)}) collective-permute-start(f32[264,256]{1,0:T(8,128)S(1)} %get-tuple-element.47.held_ref), channel_id=1, source_target_pairs={{0,8},{2,10},{4,12},{6,14},{8,0},{10,2},{12,4},{14,6},{16,24},{18,... | collective-permute-start | bytes 811016 | tf_op jit(solution)/shard_map/ppermute | solution.py:272
  29.5 4.9 %collective-permute-done.12 = f32[264,256]{1,0:T(8,128)S(1)} collective-permute-done((f32[264,256]{1,0:T(8,128)S(1)}, f32[264,256]{1,0:T(8,128)S(1)}, u32[]{:S(2)}, u32[]{:S(2)}) %collective-permute-start.12) | collective-permute-done | bytes 270368 | tf_op jit(solution)/shard_map/ppermute | solution.py:272
  34.4 2.0 %collective-permute-start.13 = (f32[264,256]{1,0:T(8,128)S(1)}, f32[264,256]{1,0:T(8,128)}, u32[]{:S(2)}, u32[]{:S(2)}) collective-permute-start(f32[264,256]{1,0:T(8,128)S(1)} %collective-permute-done.12), channel_id=1, source_target_pairs={{0,1},{2,3},{4,5},{6,7},{8,9},{10,11},{12,13},{14,15},{16,17},{18,... | collective-permute-start | bytes 811016 | tf_op jit(solution)/shard_map/ppermute | solution.py:272
  39.3 7.4 %shard_map.85 = (f32[640,256]{1,0:T(8,128)S(1)}, f32[640,256]{1,0:T(8,128)}, f32[512,1024]{1,0:T(8,128)}, f32[512,256]{1,0:T(8,128)}) custom-call(s32[1]{0:T(128)} %bitcast.me_ref, f32[512,1024]{1,0:T(8,128)S(1)} %copy-done, f32[512,256]{1,0:T(8,128)S(1)} %copy-done.7, f32[256,256]{1,0:T(8,128)S(1)} %copy-done.10, f32[256,256]{1,0:T(8,128)S(1)} %copy-done.3), custom_call_target="tpu_custom_call" | custom-call | tf_op jit(solution)/shard_map/pallas_call | solution.py:306
  54.9 1.9 %collective-permute-start.4 = (f32[160,256]{1,0:T(8,128)S(1)}, f32[160,256]{1,0:T(8,128)S(1)}, u32[]{:S(2)}, u32[]{:S(2)}) collective-permute-start(f32[160,256]{1,0:T(8,128)S(1)} %get-tuple-element.30), channel_id=1, source_target_pairs={{0,6},{1,7},{2,4},{3,5},{4,2},{5,3},{6,0},{7,1},{8,14},{9,15},{10,... | collective-permute-start | bytes 491528 | tf_op jit(solution)/shard_map/ppermute | solution.py:272
  56.8 4.1 %collective-permute-done.15 = f32[264,256]{1,0:T(8,128)} collective-permute-done((f32[264,256]{1,0:T(8,128)S(1)}, f32[264,256]{1,0:T(8,128)}, u32[]{:S(2)}, u32[]{:S(2)}) %collective-permute-start.15) | collective-permute-done | bytes 270368 | tf_op jit(solution)/shard_map/ppermute | solution.py:272
  60.9 2.0 %collective-permute-start.16 = (f32[264,256]{1,0:T(8,128)}, f32[264,256]{1,0:T(8,128)}, u32[]{:S(2)}, u32[]{:S(2)}) collective-permute-start(f32[264,256]{1,0:T(8,128)} %collective-permute-done.15), channel_id=1, source_target_pairs={{0,1},{2,3},{4,5},{6,7},{8,9},{10,11},{12,13},{14,15},{16,17},{18,... | collective-permute-start | bytes 811016 | tf_op jit(solution)/shard_map/ppermute | solution.py:272
  63.7 1.9 %shard_map.88 = (f32[128,256]{1,0:T(8,128)S(1)}, f32[160,256]{1,0:T(8,128)S(1)}, f32[4,128,256]{2,1,0:T(8,128)S(1)}) custom-call(s32[1]{0:T(128)} %bitcast.me_ref, f32[160,256]{1,0:T(8,128)S(1)} %get-tuple-element.27.refs_0_, f32[160,256]{1,0:T(8,128)S(1)} %collective-permute-done.2.refs_1_, f32[160,256]{1,0:T(8,128)S(1)} %collective-permute-done.3.refs_2_, ...), custom_call_target="tpu_custom_call" | custom-call | tf_op jit(solution)/shard_map/pallas_call | solution.py:284
  65.6 1.7 %collective-permute-start.11 = (f32[160,256]{1,0:T(8,128)S(1)}, f32[160,256]{1,0:T(8,128)S(1)}, u32[]{:S(2)}, u32[]{:S(2)}) collective-permute-start(f32[160,256]{1,0:T(8,128)S(1)} %get-tuple-element.32.mine_ref), channel_id=1, source_target_pairs={{0,8},{1,9},{2,10},{3,11},{4,12},{5,13},{6,14},{7,15},{8,0},{9,1},... | collective-permute-start | bytes 491528 | tf_op jit(solution)/shard_map/ppermute | solution.py:272
  67.3 4.0 %collective-permute-done.11.there_ref = f32[160,256]{1,0:T(8,128)S(1)} collective-permute-done((f32[160,256]{1,0:T(8,128)S(1)}, f32[160,256]{1,0:T(8,128)S(1)}, u32[]{:S(2)}, u32[]{:S(2)}) %collective-permute-start.11) | collective-permute-done | bytes 163872 | tf_op jit(solution)/shard_map/ppermute | solution.py:272
  71.9 2.6 %collective-permute-start.14 = (f32[160,256]{1,0:T(8,128)S(1)}, f32[160,256]{1,0:T(8,128)S(1)}, u32[]{:S(2)}, u32[]{:S(2)}) collective-permute-start(f32[160,256]{1,0:T(8,128)S(1)} %get-tuple-element.35.mine_ref), channel_id=1, source_target_pairs={{0,16},{1,17},{2,18},{3,19},{4,20},{5,21},{6,22},{7,23},{8,24},{9,... | collective-permute-start | bytes 491528 | tf_op jit(solution)/shard_map/ppermute | solution.py:272
  75.5 5.5 %collective-permute-done.14.there_ref = f32[160,256]{1,0:T(8,128)S(1)} collective-permute-done((f32[160,256]{1,0:T(8,128)S(1)}, f32[160,256]{1,0:T(8,128)S(1)}, u32[]{:S(2)}, u32[]{:S(2)}) %collective-permute-start.14) | collective-permute-done | bytes 163872 | tf_op jit(solution)/shard_map/ppermute | solution.py:272
  82.3 1.6 %collective-permute-start.18 = (f32[192,256]{1,0:T(8,128)S(1)}, f32[192,256]{1,0:T(8,128)S(1)}, u32[]{:S(2)}, u32[]{:S(2)}) collective-permute-start(f32[192,256]{1,0:T(8,128)S(1)} %get-tuple-element.39), channel_id=1, source_target_pairs={{0,4},{1,5},{2,6},{3,7},{4,0},{5,1},{6,2},{7,3},{8,12},{9,13},{10,... | collective-permute-start | bytes 589832 | tf_op jit(solution)/shard_map/ppermute | solution.py:272
  85.3 4.3 %collective-permute-done.17.refs_1_ = f32[192,256]{1,0:T(8,128)S(1)} collective-permute-done((f32[192,256]{1,0:T(8,128)S(1)}, f32[192,256]{1,0:T(8,128)S(1)}, u32[]{:S(2)}, u32[]{:S(2)}) %collective-permute-start.17) | collective-permute-done | bytes 196640 | tf_op jit(solution)/shard_map/ppermute | solution.py:272
  91.1 1.8 %collective-permute-done.19.refs_3_ = f32[192,256]{1,0:T(8,128)S(1)} collective-permute-done((f32[192,256]{1,0:T(8,128)S(1)}, f32[192,256]{1,0:T(8,128)S(1)}, u32[]{:S(2)}, u32[]{:S(2)}) %collective-permute-start.19) | collective-permute-done | bytes 196640 | tf_op jit(solution)/shard_map/ppermute | solution.py:272
  93.1 2.3 %collective-permute-done.20.refs_8_ = f32[4,192,256]{2,1,0:T(8,128)S(1)} collective-permute-done((f32[4,192,256]{2,1,0:T(8,128)S(1)}, f32[4,192,256]{2,1,0:T(8,128)S(1)}, u32[]{:S(2)}, u32[]{:S(2)}) %collective-permute-start.20) | collective-permute-done | bytes 786464 | tf_op jit(solution)/shard_map/ppermute | solution.py:272
  95.4 2.5 %shard_map.92 = (f32[512,1024]{1,0:T(8,128)}, f32[512,256]{1,0:T(8,128)}, f32[256,256]{1,0:T(8,128)}) custom-call(s32[1]{0:T(128)} %bitcast.me_ref, f32[192,256]{1,0:T(8,128)S(1)} %get-tuple-element.37.refs_0_, f32[192,256]{1,0:T(8,128)S(1)} %collective-permute-done.17.refs_1_, ...), custom_call_target="tpu_custom_call", output_to_operand_aliasing={{0}: (11, {}), {1}: (12, {})} | custom-call | tf_op jit(solution)/shard_map/pallas_call | solution.py:380
  (57 shorter events, 23.3 us)
Async XLA Ops:
  2.7 33.7 %copy-start = (f32[512,1024]{1,0:T(8,128)S(1)}, f32[512,1024]{1,0:T(8,128)}, u32[]{:S(2)}) copy-start(f32[512,1024]{1,0:T(8,128)} %trailing_ref.1) | copy-start | bytes 6291460
  2.7 10.4 %collective-permute-start.7 = (f32[264,256]{1,0:T(8,128)S(1)}, f32[264,256]{1,0:T(8,128)}, u32[]{:S(2)}, u32[]{:S(2)}) collective-permute-start(f32[264,256]{1,0:T(8,128)S(1)} %shard_map.86), channel_id=1, source_target_pairs={{0,4},{2,6},{4,0},{6,2},{8,12},{10,14},{12,8},{14,10},{16,20},{18,... | collective-permute-start | bytes 811016 | tf_op jit(solution)/shard_map/ppermute | solution.py:272
  7.7 8.5 %collective-permute-start.5 = (f32[264,256]{1,0:T(8,128)S(1)}, f32[264,256]{1,0:T(8,128)}, u32[]{:S(2)}, u32[]{:S(2)}) collective-permute-start(f32[264,256]{1,0:T(8,128)S(1)} %shard_map.86), channel_id=1, source_target_pairs={{0,2},{2,0},{4,6},{6,4},{8,10},{10,8},{12,14},{14,12},{16,18},{18,... | collective-permute-start | bytes 811016 | tf_op jit(solution)/shard_map/ppermute | solution.py:272
  11.1 9.4 %collective-permute-start.9 = (f32[264,256]{1,0:T(8,128)S(1)}, f32[264,256]{1,0:T(8,128)}, u32[]{:S(2)}, u32[]{:S(2)}) collective-permute-start(f32[264,256]{1,0:T(8,128)S(1)} %shard_map.86), channel_id=1, source_target_pairs={{0,6},{2,4},{4,2},{6,0},{8,14},{10,12},{12,10},{14,8},{16,22},{18,... | collective-permute-start | bytes 811016 | tf_op jit(solution)/shard_map/ppermute | solution.py:272
  13.0 9.4 %collective-permute-start.1 = (f32[264,256]{1,0:T(8,128)S(1)}, f32[264,256]{1,0:T(8,128)}, u32[]{:S(2)}, u32[]{:S(2)}) collective-permute-start(f32[264,256]{1,0:T(8,128)S(1)} %shard_map.86), channel_id=1, source_target_pairs={{0,1},{1,0},{2,3},{3,2},{4,5},{5,4},{6,7},{7,6},{8,9},{9,8},{10,11... | collective-permute-start | bytes 811016 | tf_op jit(solution)/shard_map/ppermute | solution.py:272
  13.1 9.3 %collective-permute-start.8 = (f32[264,256]{1,0:T(8,128)}, f32[264,256]{1,0:T(8,128)S(1)}, u32[]{:S(2)}, u32[]{:S(2)}) collective-permute-start(f32[264,256]{1,0:T(8,128)} %collective-permute-done.7), channel_id=1, source_target_pairs={{0,1},{2,3},{4,5},{6,7},{8,9},{10,11},{12,13},{14,15},{16,17},{18,... | collective-permute-start | bytes 811016 | tf_op jit(solution)/shard_map/ppermute | solution.py:272
  16.1 6.3 %collective-permute-start.6 = (f32[264,256]{1,0:T(8,128)}, f32[264,256]{1,0:T(8,128)S(1)}, u32[]{:S(2)}, u32[]{:S(2)}) collective-permute-start(f32[264,256]{1,0:T(8,128)} %collective-permute-done.5), channel_id=1, source_target_pairs={{0,1},{2,3},{4,5},{6,7},{8,9},{10,11},{12,13},{14,15},{16,17},{18,... | collective-permute-start | bytes 811016 | tf_op jit(solution)/shard_map/ppermute | solution.py:272
  20.5 3.4 %collective-permute-start.10 = (f32[264,256]{1,0:T(8,128)}, f32[264,256]{1,0:T(8,128)}, u32[]{:S(2)}, u32[]{:S(2)}) collective-permute-start(f32[264,256]{1,0:T(8,128)} %collective-permute-done.9), channel_id=1, source_target_pairs={{0,1},{2,3},{4,5},{6,7},{8,9},{10,11},{12,13},{14,15},{16,17},{18,... | collective-permute-start | bytes 811016 | tf_op jit(solution)/shard_map/ppermute | solution.py:272
  26.0 8.3 %collective-permute-start.12 = (f32[264,256]{1,0:T(8,128)S(1)}, f32[264,256]{1,0:T(8,128)S(1)}, u32[]{:S(2)}, u32[]{:S(2)}) collective-permute-start(f32[264,256]{1,0:T(8,128)S(1)} %get-tuple-element.47.held_ref), channel_id=1, source_target_pairs={{0,8},{2,10},{4,12},{6,14},{8,0},{10,2},{12,4},{14,6},{16,24},{18,... | collective-permute-start | bytes 811016 | tf_op jit(solution)/shard_map/ppermute | solution.py:272
  34.4 13.2 %collective-permute-start.13 = (f32[264,256]{1,0:T(8,128)S(1)}, f32[264,256]{1,0:T(8,128)}, u32[]{:S(2)}, u32[]{:S(2)}) collective-permute-start(f32[264,256]{1,0:T(8,128)S(1)} %collective-permute-done.12), channel_id=1, source_target_pairs={{0,1},{2,3},{4,5},{6,7},{8,9},{10,11},{12,13},{14,15},{16,17},{18,... | collective-permute-start | bytes 811016 | tf_op jit(solution)/shard_map/ppermute | solution.py:272
  47.5 16.2 %copy-start.1 = (f32[264,256]{1,0:T(8,128)S(1)}, f32[264,256]{1,0:T(8,128)}, u32[]{:S(2)}) copy-start(f32[264,256]{1,0:T(8,128)} %get-tuple-element.51.refs_4_) | copy-start | bytes 811012
  47.5 2.4 %collective-permute-start = (f32[640,256]{1,0:T(8,128)}, f32[640,256]{1,0:T(8,128)S(1)}, u32[]{:S(2)}, u32[]{:S(2)}) collective-permute-start(f32[640,256]{1,0:T(8,128)} %get-tuple-element.26), channel_id=1, source_target_pairs={{0,1},{1,0},{2,3},{3,2},{4,5},{5,4},{6,7},{7,6},{8,9},{9,8},{10,11... | collective-permute-start | bytes 1966088 | tf_op jit(solution)/shard_map/ppermute | solution.py:272
  48.6 12.3 %collective-permute-start.15 = (f32[264,256]{1,0:T(8,128)S(1)}, f32[264,256]{1,0:T(8,128)}, u32[]{:S(2)}, u32[]{:S(2)}) collective-permute-start(f32[264,256]{1,0:T(8,128)S(1)} %get-tuple-element.52.next_ref.held_ref), channel_id=1, source_target_pairs={{16,0},{18,2},{20,4},{22,6},{24,8},{26,10},{28,12},{30,14}} | collective-permute-start | bytes 811016 | tf_op jit(solution)/shard_map/ppermute | solution.py:272
  53.3 9.6 %collective-permute-start.2 = (f32[160,256]{1,0:T(8,128)S(1)}, f32[160,256]{1,0:T(8,128)S(1)}, u32[]{:S(2)}, u32[]{:S(2)}) collective-permute-start(f32[160,256]{1,0:T(8,128)S(1)} %get-tuple-element.28), channel_id=1, source_target_pairs={{0,2},{1,3},{2,0},{3,1},{4,6},{5,7},{6,4},{7,5},{8,10},{9,11},{10,... | collective-permute-start | bytes 491528 | tf_op jit(solution)/shard_map/ppermute | solution.py:272
  53.9 9.9 %collective-permute-start.3 = (f32[160,256]{1,0:T(8,128)S(1)}, f32[160,256]{1,0:T(8,128)S(1)}, u32[]{:S(2)}, u32[]{:S(2)}) collective-permute-start(f32[160,256]{1,0:T(8,128)S(1)} %get-tuple-element.29), channel_id=1, source_target_pairs={{0,4},{1,5},{2,6},{3,7},{4,0},{5,1},{6,2},{7,3},{8,12},{9,13},{10,... | collective-permute-start | bytes 491528 | tf_op jit(solution)/shard_map/ppermute | solution.py:272
  54.9 8.8 %collective-permute-start.4 = (f32[160,256]{1,0:T(8,128)S(1)}, f32[160,256]{1,0:T(8,128)S(1)}, u32[]{:S(2)}, u32[]{:S(2)}) collective-permute-start(f32[160,256]{1,0:T(8,128)S(1)} %get-tuple-element.30), channel_id=1, source_target_pairs={{0,6},{1,7},{2,4},{3,5},{4,2},{5,3},{6,0},{7,1},{8,14},{9,15},{10,... | collective-permute-start | bytes 491528 | tf_op jit(solution)/shard_map/ppermute | solution.py:272
  60.9 13.5 %collective-permute-start.16 = (f32[264,256]{1,0:T(8,128)}, f32[264,256]{1,0:T(8,128)}, u32[]{:S(2)}, u32[]{:S(2)}) collective-permute-start(f32[264,256]{1,0:T(8,128)} %collective-permute-done.15), channel_id=1, source_target_pairs={{0,1},{2,3},{4,5},{6,7},{8,9},{10,11},{12,13},{14,15},{16,17},{18,... | collective-permute-start | bytes 811016 | tf_op jit(solution)/shard_map/ppermute | solution.py:272
  65.6 5.6 %collective-permute-start.11 = (f32[160,256]{1,0:T(8,128)S(1)}, f32[160,256]{1,0:T(8,128)S(1)}, u32[]{:S(2)}, u32[]{:S(2)}) collective-permute-start(f32[160,256]{1,0:T(8,128)S(1)} %get-tuple-element.32.mine_ref), channel_id=1, source_target_pairs={{0,8},{1,9},{2,10},{3,11},{4,12},{5,13},{6,14},{7,15},{8,0},{9,1},... | collective-permute-start | bytes 491528 | tf_op jit(solution)/shard_map/ppermute | solution.py:272
  71.9 9.1 %collective-permute-start.14 = (f32[160,256]{1,0:T(8,128)S(1)}, f32[160,256]{1,0:T(8,128)S(1)}, u32[]{:S(2)}, u32[]{:S(2)}) collective-permute-start(f32[160,256]{1,0:T(8,128)S(1)} %get-tuple-element.35.mine_ref), channel_id=1, source_target_pairs={{0,16},{1,17},{2,18},{3,19},{4,20},{5,21},{6,22},{7,23},{8,24},{9,... | collective-permute-start | bytes 491528 | tf_op jit(solution)/shard_map/ppermute | solution.py:272
  75.5 19.9 %copy-start.4 = (f32[256,256]{1,0:T(8,128)S(1)}, f32[256,256]{1,0:T(8,128)}, u32[]{:S(2)}) copy-start(f32[256,256]{1,0:T(8,128)} %refs_9_.1) | copy-start | bytes 786436
  81.7 7.9 %collective-permute-start.17 = (f32[192,256]{1,0:T(8,128)S(1)}, f32[192,256]{1,0:T(8,128)S(1)}, u32[]{:S(2)}, u32[]{:S(2)}) collective-permute-start(f32[192,256]{1,0:T(8,128)S(1)} %get-tuple-element.38), channel_id=1, source_target_pairs={{0,2},{1,3},{2,0},{3,1},{4,6},{5,7},{6,4},{7,5},{8,10},{9,11},{10,... | collective-permute-start | bytes 589832 | tf_op jit(solution)/shard_map/ppermute | solution.py:272
  82.3 8.8 %collective-permute-start.18 = (f32[192,256]{1,0:T(8,128)S(1)}, f32[192,256]{1,0:T(8,128)S(1)}, u32[]{:S(2)}, u32[]{:S(2)}) collective-permute-start(f32[192,256]{1,0:T(8,128)S(1)} %get-tuple-element.39), channel_id=1, source_target_pairs={{0,4},{1,5},{2,6},{3,7},{4,0},{5,1},{6,2},{7,3},{8,12},{9,13},{10,... | collective-permute-start | bytes 589832 | tf_op jit(solution)/shard_map/ppermute | solution.py:272
  83.9 9.0 %collective-permute-start.19 = (f32[192,256]{1,0:T(8,128)S(1)}, f32[192,256]{1,0:T(8,128)S(1)}, u32[]{:S(2)}, u32[]{:S(2)}) collective-permute-start(f32[192,256]{1,0:T(8,128)S(1)} %get-tuple-element.40), channel_id=1, source_target_pairs={{0,6},{1,7},{2,4},{3,5},{4,2},{5,3},{6,0},{7,1},{8,14},{9,15},{10,... | collective-permute-start | bytes 589832 | tf_op jit(solution)/shard_map/ppermute | solution.py:272
  93.0 2.4 %collective-permute-start.20 = (f32[4,192,256]{2,1,0:T(8,128)S(1)}, f32[4,192,256]{2,1,0:T(8,128)S(1)}, u32[]{:S(2)}, u32[]{:S(2)}) collective-permute-start(f32[4,192,256]{2,1,0:T(8,128)S(1)} %shard_map.91), channel_id=1, source_target_pairs={{0,1},{1,0},{2,3},{3,2},{4,5},{5,4},{6,7},{7,6},{8,9},{9,8},{10,11... | collective-permute-start | bytes 2359304 | tf_op jit(solution)/shard_map/ppermute | solution.py:272
  (11 other events, 22.3 us)
where the time goes:
time: 98.5 us; the launch traced here: 97.9 us
  starting transfers between devices  36.2 us (37%)
  waiting for transfers between devices  32.9 us (33%)
  Pallas kernels  14.5 us (15%)
  local copies, waits for them, and re-layouts  9.14 us (9%)
  other arithmetic  4.24 us (4%)
    ppermute x21, starting transfers between devices, exchange(): return lax.ppermute(value, 'rows', pairs)  36.2 us
    ppermute x21, waiting for transfers between devices, exchange(): return lax.ppermute(value, 'rows', pairs)  32.9 us
    unnamed x28, local copies, waits for them, and re-layouts  9.14 us
    pallas_call x1, Pallas kernels, body(): pl.pallas_call(leaf_kernel, grid=(count,), out_shape=(shape(leaf_rows, wi...  7.38 us
    pallas_call x5, Pallas kernels, whole_call(): pl.pallas_call(kernel, out_shape=outs, in_specs=[SCALAR] + [WHOLE] * len(...  4.51 us
    pallas_call x1, Pallas kernels, body(): pl.pallas_call(functools.partial(final_kernel, total=float(rows * devices...  2.5 us
    select_n x1, other arithmetic, by_place(): out = jnp.where(source == r, parts[r], out)  2.15 us
  transfers between devices with their start and end apart: 21, of which 11 were waited for; matrix products, arithmetic and copies ran while one was open for 2% of the time, Pallas kernels for 11%

commit v1 on v0

v1 whole, which is shorter than its diff:
```python
import functools
import jax
import jax.numpy as jnp
from jax import lax
from jax.experimental import pallas as pl
from jax.experimental.pallas import tpu as pltpu
from jax.sharding import PartitionSpec as P

F32 = jnp.float32
BF16 = jnp.bfloat16
EXTRA = 8
PARAMS = pltpu.CompilerParams(vmem_limit_bytes=40 * 1024 * 1024)
def room(megabytes):
    return pltpu.CompilerParams(vmem_limit_bytes=megabytes * 1024 * 1024)


WHOLE = pl.BlockSpec(memory_space=pltpu.VMEM)
SCALAR = pl.BlockSpec(memory_space=pltpu.SMEM)
AWAY = pl.BlockSpec(memory_space=pltpu.HBM)


def halves(value):
    high = value.astype(BF16)
    return high, (value - high.astype(F32)).astype(BF16)


def times(left, right, sides):
    dims = ((sides[:1], sides[1:]), ((), ()))
    dot = functools.partial(lax.dot_general, dimension_numbers=dims, preferred_element_type=F32)
    return dot(left[0], right[0]) + (dot(left[0], right[1]) + dot(left[1], right[0]))


def plain(left, right):
    return times(left, right, (1, 0))


def by_transpose(left, right):
    return times(left, right, (1, 1))


def pack_kernel(vectors_hbm, factors_hbm, out_ref, vectors_ref, factors_ref, sems):
    copies = [
        pltpu.make_async_copy(vectors_hbm, vectors_ref, sems.at[0]),
        pltpu.make_async_copy(factors_hbm, factors_ref, sems.at[1]),
    ]
    for copy in copies:
        copy.start()
    for copy in copies:
        copy.wait()
    width = vectors_ref.shape[0]
    half = width // 2
    row = lax.broadcasted_iota(jnp.int32, (width, width), 0)
    col = lax.broadcasted_iota(jnp.int32, (width, width), 1)
    factors = factors_ref[...]
    packed = jnp.where(row > col, factors.T, vectors_ref[...])
    diagonal = jnp.sum(jnp.where(row == col, factors, 0.0), axis=0, keepdims=True)
    for part in range(2):
        out_ref[part, :half] = packed[part * half : (part + 1) * half]
        out_ref[part, half:] = jnp.broadcast_to(diagonal, (EXTRA, width))


def unpack(first, second):
    half = first.shape[0] - EXTRA
    width = 2 * half
    packed = jnp.concatenate([first[:half], second[:half]], axis=0)
    row = lax.broadcasted_iota(jnp.int32, (width, width), 0)
    col = lax.broadcasted_iota(jnp.int32, (width, width), 1)
    diagonal = jnp.broadcast_to(first[half : half + 1], (width, width))
    vectors = jnp.where(row <= col, packed, 0.0)
    factors = jnp.where(row > col, packed, jnp.where(row == col, diagonal, 0.0))
    return halves(vectors), halves(factors)


def by_core(core, mine, there):
    odd = core == 1
    return jnp.where(odd, there, mine), jnp.where(odd, mine, there)


def place(me):
    return (me >> 1) & 3


def by_place(me, parts, wanted):
    source = place(me) ^ wanted
    out = parts[0]
    for r in range(1, 4):
        out = jnp.where(source == r, parts[r], out)
    return out


def tree_node(low, high, reflector):
    vectors, factors = reflector
    node = by_transpose(halves(low + plain(halves(high), vectors)), factors)
    return low - node, high - by_transpose(halves(node), vectors)


def leaf_kernel(
    me_ref, trailing_hbm, vectors_hbm, factors_hbm, inverse_hbm,
    own_hbm, away_hbm, updated_hbm, basis_hbm,
    own_ref, away_ref, part_ref, vectors_ref, factors_ref, inverse_ref, rest_ref, basis_ref, head_ref, gram_ref,
    in_sems, out_sems,
):
    count, rows, width = part_ref.shape
    half = width // 2
    core = me_ref[0] % 2
    mine = pl.ds(pl.multiple_of(core * half, half), half)
    other = pl.ds(pl.multiple_of((1 - core) * half, half), half)

    copies = []

    def fetch(source, target):
        copy = pltpu.make_async_copy(source, target, in_sems.at[len(copies)])
        copy.start()
        copies.append(copy)
        return copy

    def fetch_part(b):
        cuts = [slice(cut, cut + width) for cut in range(0, rows, width)]
        return [fetch(trailing_hbm.at[cut, pl.ds(b * width, width)], part_ref.at[b, cut]) for cut in cuts]

    parts = [fetch_part(0)]
    vectors_copy = fetch(vectors_hbm, vectors_ref)
    factors_copy = fetch(factors_hbm, factors_ref)
    inverse_copy = fetch(inverse_hbm, inverse_ref)
    parts += [fetch_part(b) for b in range(1, count)]

    out_copies = []

    def put(source, target):
        copy = pltpu.make_async_copy(source, target, out_sems.at[len(out_copies)])
        copy.start()
        out_copies.append(copy)

    for b in range(count):
        for copy in parts[b]:
            copy.wait()
        part = part_ref[b].T
        split = halves(part)
        if b == 0:
            gram_ref[...] = by_transpose(split, split)
            rows_b = slice(count * half, (count + 1) * half)
            own_ref[rows_b] = gram_ref[mine]
            away_ref[rows_b] = gram_ref[other]
            put(away_ref.at[rows_b], away_hbm.at[rows_b])
            put(own_ref.at[rows_b], own_hbm.at[rows_b])
            vectors_copy.wait()
            vectors = halves(vectors_ref[...])
            factors_copy.wait()
            factors = halves(factors_ref[...])
        coeffs = plain(halves(plain(split, vectors)), factors)
        out = part - by_transpose(halves(coeffs), vectors)
        head_ref[...] = out[:, :width]
        rows_b = slice(b * half, (b + 1) * half)
        own_ref[rows_b] = head_ref[mine]
        away_ref[rows_b] = head_ref[other]
        put(away_ref.at[rows_b], away_hbm.at[rows_b])
        put(own_ref.at[rows_b], own_hbm.at[rows_b])
        rest = out[:, width:].T
        rest_ref[b] = rest
        put(rest_ref.at[b], updated_hbm.at[pl.ds(width, width), pl.ds(b * width, width)])
        if b == 0:
            inverse_copy.wait()
            basis_ref[...] = plain(halves(rest), halves(inverse_ref[...]))
            put(basis_ref, basis_hbm.at[pl.ds(width, width)])
    for copy in out_copies:
        copy.wait()


def core_kernel(
    me_ref, own_ref, there_ref, packed_ref, packed_there_ref, *refs
):
    sends, dones, (low_ref, high_ref) = refs[:4], refs[4:8], refs[8:]
    me = me_ref[0]
    width = own_ref.shape[1]
    half = width // 2
    quarter = half // 4
    count = own_ref.shape[0] // half - 1
    odd = me % 2 == 1
    mine, there = own_ref[: count * half], there_ref[: count * half]
    low = jnp.where(odd, there, mine)
    high = jnp.where(odd, mine, there)
    first, second = [jnp.where(odd, packed_ref[part], packed_there_ref[part]) for part in range(2)]
    low, high = tree_node(low, high, unpack(first, second))
    low_ref[: count * half] = low
    low_ref[count * half :] = own_ref[count * half :] + there_ref[count * half :]
    high_ref[...] = high
    for r in range(4):
        start = (place(me) ^ r) * quarter
        for b in range(count + 1):
            source = pl.ds(pl.multiple_of(b * half + start, quarter), quarter)
            target = slice(b * quarter, (b + 1) * quarter)
            sends[r][target] = low_ref[source]
            if b < count:
                dones[r][target] = high_ref[source]


def gather_kernel(me_ref, *refs):
    parts, own_hbm, (stack_ref, held_ref, own_ref, sem) = refs[:4], refs[4], refs[5:]
    copy = pltpu.make_async_copy(own_hbm, own_ref, sem)
    copy.start()
    for r in range(1, 4):
        stack_ref[r - 1] = parts[r][...]
    held_ref[...] = by_place(me_ref[0], [ref[...] for ref in parts], 0)
    copy.wait()


def plane_kernel(
    me_ref, *refs, level
):
    gots, (packed_ref, packed_there_ref, stack_ref, stack_there_ref) = refs[:4], refs[4:8]
    head_ref, send_ref, done_ref, held_ref = refs[8:]
    me = me_ref[0]
    core = me % 2
    cols = done_ref.shape[1]
    odd = core == 1
    pairs = [[jnp.where(odd, packed_there_ref[part], packed_ref[part]) for part in range(2)]]
    pairs += [by_core(core, stack_ref[r], stack_there_ref[r]) for r in range(3)]
    firsts, seconds = [pair[0] for pair in pairs], [pair[1] for pair in pairs]
    pairs = [(by_place(me, firsts, j), by_place(me, seconds, j)) for j in range(4)]
    held_ref[0], held_ref[1] = pairs[0]
    reflectors = [unpack(*pair) for pair in pairs]
    parts = [ref[:cols] for ref in gots]
    heads = [by_place(me, parts, j) for j in range(4)]
    gram = gots[0][cols:] + gots[1][cols:] + (gots[2][cols:] + gots[3][cols:])
    heads[0], heads[1] = tree_node(heads[0], heads[1], reflectors[1])
    heads[2], heads[3] = tree_node(heads[2], heads[3], reflectors[3])
    heads[0], heads[2] = tree_node(heads[0], heads[2], reflectors[2])
    for j in range(4):
        done_ref[j] = heads[j]
    head_ref[...] = heads[0]
    upper = (me >> level) % 2 == 1
    send_ref[:cols] = jnp.where(upper, plain(halves(heads[0]), reflectors[0][0]), heads[0])
    send_ref[cols:] = gram


def line_node(
    me, head_ref, result_ref, mine_ref, there_ref, held_ref, part_ref, part_there_ref, level
):
    cols = head_ref.shape[0]
    upper = (me >> level) % 2 == 1
    held = held_ref[0], held_ref[1]
    others = by_core(me % 2, part_ref[...], part_there_ref[...])
    node = [jnp.where(upper, a, b) for a, b in zip(held, others)]
    following = [jnp.where(upper, b, a) for a, b in zip(held, others)]
    head = head_ref[...]
    there = there_ref[:cols]
    coeffs = by_transpose(halves(mine_ref[:cols] + there), unpack(*node)[1])
    low = jnp.where(upper, there, head) - coeffs
    plane = me >> 3
    below = (1 << (level - 2)) - 1
    second = (plane & below) == (1 << (level - 3))
    high = head - by_transpose(halves(coeffs), unpack(*held)[0])
    result = jnp.where(second, high, result_ref[...])
    return low, result, mine_ref[cols:] + there_ref[cols:], following


def line_kernel(me_ref, *refs, level):
    head_out, result_out, send_ref, held_out = refs[7:]
    me = me_ref[0]
    low, result, gram, following = line_node(me, *refs[:7], level)
    cols = low.shape[0]
    ahead = (me >> (level + 1)) % 2 == 1
    head_out[...] = low
    result_out[...] = result
    held_out[0], held_out[1] = following
    send_ref[:cols] = jnp.where(ahead, plain(halves(low), unpack(*following)[0]), low)
    send_ref[cols:] = gram


def last_kernel(me_ref, *refs, level):
    done_ref, sends, all_ref = refs[7], refs[8:12], refs[12]
    me = me_ref[0]
    low, result, gram, _ = line_node(me, *refs[:7], level)
    cols = low.shape[0]
    quarter = gram.shape[0]
    all_ref[0] = jnp.where((me >> 3) == 0, low, result)
    for j in range(1, 4):
        all_ref[j] = done_ref[j]
    for r in range(4):
        sends[r][:cols] = all_ref[place(me) ^ r]
        sends[r][cols : cols + quarter] = low[:quarter]
        sends[r][cols + quarter :] = gram


def pass_kernel(me_ref, *refs):
    backs, dones, out_ref = refs[:4], refs[4:8], refs[8]
    odd = me_ref[0] % 2 == 1
    cols = dones[0].shape[0]
    for r in range(4):
        out_ref[r, :cols] = jnp.where(odd, backs[r][:cols], dones[r][...])
        out_ref[r, cols:] = backs[r][cols:]


def final_kernel(me_ref, *refs, total):
    backs, dones = refs[:4], refs[4:8]
    there_ref, inverse_hbm, _, _, updated_hbm, basis_hbm, gram_ref = refs[8:15]
    head_ref, panel_ref, sum_ref, inverse_ref, out_ref, basis_ref, sems = refs[15:]
    count, width = out_ref.shape[:2]
    half = width // 2
    quarter = half // 4
    cols = count * quarter
    me = me_ref[0]
    core = me % 2
    odd = core == 1
    copy = pltpu.make_async_copy(inverse_hbm, inverse_ref, sems.at[0])
    copy.start()

    def target(part, r):
        return pl.ds(pl.multiple_of(part * half + (place(me) ^ r) * quarter, quarter), quarter)

    copies = []

    def put(source, place_there):
        copies.append(pltpu.make_async_copy(source, place_there, sems.at[len(copies) + 1]))
        copies[-1].start()

    for b in range(count):
        rows = slice(b * quarter, (b + 1) * quarter)
        for r in range(4):
            there = there_ref[r, rows]
            head_ref[b, target(0, r)] = jnp.where(odd, there, backs[r][rows])
            head_ref[b, target(1, r)] = jnp.where(odd, dones[r][rows], there)
        out_ref[b] = head_ref[b].T
        put(out_ref.at[b], updated_hbm.at[pl.ds(0, width), pl.ds(b * width, width)])
        if b == 0:
            copy.wait()
            basis = plain(halves(out_ref[0]), halves(inverse_ref[...]))
            basis_ref[...] = jnp.where(me == 0, 0.0, basis)
            put(basis_ref, basis_hbm.at[pl.ds(0, width)])
    for r in range(4):
        panel_ref[target(core, r)] = backs[r][cols : cols + quarter]
        sum_ref[target(core, r)] = backs[r][cols + quarter :]
        panel_ref[target(1 - core, r)] = there_ref[r, cols : cols + quarter]
        sum_ref[target(1 - core, r)] = there_ref[r, cols + quarter :]
    panel = halves(panel_ref[...])
    gram_ref[...] = (sum_ref[...] - by_transpose(panel, panel)) / total
    for copy in copies:
        copy.wait()


def after(value, *others):
    return lax.optimization_barrier((value, *others))[0]


def body(trailing, leaf_vectors, leaf_factors, tree_vectors, tree_factors, inverse_factor):
    rows, columns = trailing.shape
    width = leaf_vectors.shape[1]
    half = width // 2
    quarter = half // 4
    count = columns // width
    cols = count * quarter
    devices = lax.axis_size("rows")
    levels = devices.bit_length() - 1
    me = lax.axis_index("rows").astype(jnp.int32)
    me_array = me.reshape(1)
    odd = me % 2 == 1

    def exchange(value, shift):
        return lax.ppermute(value, "rows", [(i, i ^ shift) for i in range(devices)])

    def shape(*dims):
        return jax.ShapeDtypeStruct(dims, F32)

    def vmem(*dims):
        return pltpu.VMEM(dims, F32)

    def cost(flops, moved=0):
        return pl.CostEstimate(flops=flops, bytes_accessed=moved, transcendentals=0)

    def whole_call(kernel, operands, outs, scratch=(), flops=0):
        return pl.pallas_call(
            kernel,
            out_shape=outs,
            in_specs=[SCALAR] + [WHOLE] * len(operands),
            out_specs=tuple(WHOLE for _ in outs),
            scratch_shapes=list(scratch),
            compiler_params=PARAMS,
            cost_estimate=cost(flops),
        )(me_array, *operands)

    packed = pl.pallas_call(
        pack_kernel,
        out_shape=shape(2, half + EXTRA, width),
        in_specs=[AWAY] * 2,
        out_specs=WHOLE,
        scratch_shapes=[vmem(width, width), vmem(width, width), pltpu.SemaphoreType.DMA((2,))],
        compiler_params=room(62),
    )(tree_vectors, tree_factors)
    packed_there = exchange(packed, 1)
    chip_part = jnp.where(odd, packed_there[1], packed[0])
    plane_parts = [exchange(chip_part, 2 * r) for r in range(1, 4)]

    leaf_rows = count * half + half
    leaf_flops = 6 * width * columns * (2 * rows + width) + 6 * width * width * (rows + width)
    own, away, updated, basis = pl.pallas_call(
        leaf_kernel,
        out_shape=(shape(leaf_rows, width), shape(leaf_rows, width), shape(rows, columns), shape(rows, width)),
        in_specs=[SCALAR] + [AWAY] * 4,
        out_specs=(AWAY,) * 4,
        scratch_shapes=[
            vmem(leaf_rows, width),
            vmem(leaf_rows, width),
            vmem(count, rows, width),
            vmem(rows, width),
            vmem(width, width),
            vmem(width, width),
            vmem(count, width, width),
            vmem(width, width),
            vmem(width, width),
            vmem(width, width),
            pltpu.SemaphoreType.DMA((count * (rows // width) + 3,)),
            pltpu.SemaphoreType.DMA((3 * count + 3,)),
        ],
        compiler_params=room(61),
        cost_estimate=cost(leaf_flops, 4 * (2 * rows * columns + 3 * rows * width)),
    )(after(me_array, chip_part), trailing, leaf_vectors, leaf_factors, inverse_factor)
    plane_parts = [after(part, own) for part in plane_parts]
    away = exchange(after(away, *plane_parts), 1)
    stack, held_part, own = pl.pallas_call(
        gather_kernel,
        out_shape=(shape(3, half + EXTRA, width), shape(half + EXTRA, width), shape(leaf_rows, width)),
        in_specs=[SCALAR] + [WHOLE] * 4 + [AWAY],
        out_specs=(WHOLE,) * 3,
        scratch_shapes=[pltpu.SemaphoreType.DMA],
        compiler_params=PARAMS,
    )(me_array, chip_part, *plane_parts, own)
    stack_there = exchange(stack, 1)

    outs = whole_call(
        core_kernel, (own, away, packed, packed_there),
        tuple([shape(cols + quarter, width)] * 4 + [shape(cols, width)] * 4),
        (vmem(leaf_rows, width), vmem(count * half, width)),
        flops=18 * width * width * count * half,
    )
    sends, dones = outs[:4], outs[4:]
    gots = [sends[0]] + [exchange(sends[r], 2 * r) for r in range(1, 4)]

    part = after(exchange(held_part, 8), sends[1]) if levels > 3 else held_part
    head, send, plane_done, held = whole_call(
        functools.partial(plane_kernel, level=3), (*gots, packed, packed_there, stack, stack_there),
        (shape(cols, width), shape(cols + quarter, width), shape(4, cols, width), shape(2, half + EXTRA, width)),
        flops=18 * width * width * cols * 3,
    )

    result = head
    for level in range(3, levels):
        part_there = exchange(part, 1)
        operands = (head, result, send, exchange(send, 1 << level), held, part, part_there)
        if level == levels - 1:
            sends = whole_call(
                functools.partial(last_kernel, level=level), (*operands, plane_done),
                tuple([shape(cols + 2 * quarter, width)] * 4), (vmem(4, cols, width),),
                flops=18 * width * width * cols,
            )
        else:
            held_part = jnp.where((me >> level) % 2 == 1, part, held_part)
            part = after(exchange(held_part, 2 << level), head)
            head, result, send, held = whole_call(
                functools.partial(line_kernel, level=level), operands,
                (shape(cols, width), shape(cols, width), shape(cols + quarter, width), shape(*held.shape)),
                flops=18 * width * width * cols,
            )

    backs = [sends[0]] + [exchange(sends[r], 2 * r) for r in range(1, 4)]
    (back,) = whole_call(pass_kernel, (*backs, *dones), (shape(4, cols + 2 * quarter, width),))
    there = exchange(back, 1)

    return pl.pallas_call(
        functools.partial(final_kernel, total=float(rows * devices)),
        out_shape=(shape(rows, columns), shape(rows, width), shape(width, width)),
        in_specs=[SCALAR] + [WHOLE] * 9 + [AWAY] * 3,
        out_specs=(AWAY, AWAY, WHOLE),
        scratch_shapes=[
            vmem(count, width, width),
            vmem(width, width),
            vmem(width, width),
            vmem(width, width),
            vmem(count, width, width),
            vmem(width, width),
            pltpu.SemaphoreType.DMA((count + 2,)),
        ],
        input_output_aliases={11: 0, 12: 1},
        compiler_params=PARAMS,
    )(me_array, *backs, *dones, there, inverse_factor, updated, basis)


def solution(mesh):
    in_specs = (
        P("rows", None),
        P("rows", None),
        P("rows", None),
        P("rows", None),
        P("rows", None),
        P(),
    )
    out_specs = (P("rows", None), P("rows", None), P())
    return jax.shard_map(body, mesh=mesh, in_specs=in_specs, out_specs=out_specs, check_vma=False)
```

time: 98.5 us -> 69.9 us (0.71)
  starting transfers between devices: 36.2 us -> 21.2 us
  local copies, waits for them, and re-layouts: 9.14 us -> 1.09 us
  waiting for transfers between devices: 32.9 us -> 28 us
  other arithmetic: 4.24 us -> 0.94 us
  Pallas kernels: 14.5 us -> 17.7 us
    ppermute x21 -> x19, starting transfers between devices: 36.2 us -> 21.2 us  [exchange(): return lax.ppermute(value, 'rows', [(i, i ^ shift) for i in range(devices)])]
    unnamed x28 -> x6, local copies, waits for them, and re-layouts: 9.14 us -> 1.09 us
    ppermute x21 -> x19, waiting for transfers between devices: 32.9 us -> 28 us  [exchange(): return lax.ppermute(value, 'rows', [(i, i ^ shift) for i in range(devices)])]
    select_n x3 -> x2, other arithmetic: 4.24 us -> 0.94 us  [the longest x1 0.92 us: body(): chip_part = jnp.where(odd, packed_there[1], packed[0])]
    pallas_call x2 -> x3, Pallas kernels: 7.51 us -> 10.7 us  [the longest x1 8.55 us: body(): pl.pallas_call(leaf_kernel, out_shape=(shape(leaf_rows, width), shape(lea...]
  transfers between devices with their start and end apart: 21 -> 19, of which waited for: 11 -> 11; matrix products, arithmetic and copies ran while one was open for 2% -> 0% of each run, Pallas kernels for 11% -> 18%
where the time goes in v1:
time: 69.9 us; the launch traced here: 69.7 us
  waiting for transfers between devices  28 us (40%)
  starting transfers between devices  21.2 us (30%)
  Pallas kernels  17.7 us (25%)
  local copies, waits for them, and re-layouts  1.09 us (2%)
  other arithmetic  0.94 us (1%)
  between operations  0.77 us (1%)
    ppermute x19, waiting for transfers between devices, exchange(): return lax.ppermute(value, 'rows', [(i, i ^ shift) for i in range(devices)])  28 us
    ppermute x19, starting transfers between devices, exchange(): return lax.ppermute(value, 'rows', [(i, i ^ shift) for i in range(devices)])  21.2 us
    pallas_call x1, Pallas kernels, body(): pl.pallas_call(leaf_kernel, out_shape=(shape(leaf_rows, width), shape(lea...  8.55 us
    pallas_call x5, Pallas kernels, whole_call(): pl.pallas_call(kernel, out_shape=outs, in_specs=[SCALAR] + [WHOLE] * len(...  4.57 us
    pallas_call x1, Pallas kernels, body(): pl.pallas_call(functools.partial(final_kernel, total=float(rows * devices...  2.39 us
    pallas_call x1, Pallas kernels, body(): pl.pallas_call(pack_kernel, out_shape=shape(2, half + EXTRA, width), in_s...  1.89 us
  transfers between devices with their start and end apart: 19, of which 11 were waited for; matrix products, arithmetic and copies ran while one was open for 0% of the time, Pallas kernels for 18%

profile of v1, /device:TPU:0, one launch (start us, length us, event | category | flops | bytes accessed | tf_op | source)
XLA Modules:
  0.0 69.7 jit_solution(14222098029304687094)
XLA Ops:
  0.6 1.9 %shard_map.85.packed_ref.refs_4_ = f32[2,136,256]{2,1,0:T(8,128)} custom-call(f32[256,256]{1,0:T(8,128)} %vectors_hbm.2, f32[256,256]{1,0:T(8,128)} %factors_hbm.2), custom_call_target="tpu_custom_call" | custom-call | tf_op jit(solution)/shard_map/pallas_call | solution.py:381
  3.0 1.4 %collective-permute-done.packed_there_ref.refs_5_ = f32[2,136,256]{2,1,0:T(8,128)S(1)} collective-permute-done((f32[2,136,256]{2,1,0:T(8,128)}, f32[2,136,256]{2,1,0:T(8,128)S(1)}, u32[]{:S(2)}, u32[]{:S(2)}) %collective-permute-start) | collective-permute-done | bytes 278560 | tf_op jit(solution)/shard_map/ppermute | solution.py:359
  5.4 3.9 %collective-permute-start.3 = (f32[136,256]{1,0:T(8,128)S(1)}, f32[136,256]{1,0:T(8,128)S(1)}, u32[]{:S(2)}, u32[]{:S(2)}) collective-permute-start(f32[136,256]{1,0:T(8,128)S(1)} %fusion.refs_0_), channel_id=1, source_target_pairs={{0,6},{1,7},{2,4},{3,5},{4,2},{5,3},{6,0},{7,1},{8,14},{9,15},{10,... | collective-permute-start | bytes 417800 | tf_op jit(solution)/shard_map/ppermute | solution.py:359
  9.9 8.5 %shard_map.86 = (f32[640,256]{1,0:T(8,128)}, f32[640,256]{1,0:T(8,128)}, f32[512,1024]{1,0:T(8,128)}, f32[512,256]{1,0:T(8,128)}) custom-call(s32[1]{0:T(128)} %bitcast.me_ref, f32[512,1024]{1,0:T(8,128)} %trailing_hbm.1, f32[512,256]{1,0:T(8,128)} %vectors_hbm.3, f32[256,256]{1,0:T(8,128)} %factors_hbm.3, f32[256,256]{1,0:T(8,128)} %refs_9_.1), custom_call_target="tpu_custom_call" | custom-call | flops 2315255808 | bytes 5767168 | tf_op jit(solution)/shard_map/pallas_call | solution.py:395
  20.9 1.3 %shard_map.88 = (f32[160,256]{1,0:T(8,128)S(1)}, f32[160,256]{1,0:T(8,128)S(1)}, f32[160,256]{1,0:T(8,128)S(1)}, f32[160,256]{1,0:T(8,128)S(1)}, f32[128,256]{1,...) custom-call(s32[1]{0:T(128)} %bitcast.me_ref, ...), custom_call_target="tpu_custom_call" | custom-call | flops 603979776 | tf_op jit(solution)/shard_map/pallas_call | solution.py:371
  22.1 2.0 %collective-permute-start.6 = (f32[160,256]{1,0:T(8,128)S(1)}, f32[160,256]{1,0:T(8,128)S(1)}, u32[]{:S(2)}, u32[]{:S(2)}) collective-permute-start(f32[160,256]{1,0:T(8,128)S(1)} %get-tuple-element.47), channel_id=1, source_target_pairs={{0,4},{1,5},{2,6},{3,7},{4,0},{5,1},{6,2},{7,3},{8,12},{9,13},{10,... | collective-permute-start | bytes 491528 | tf_op jit(solution)/shard_map/ppermute | solution.py:359
  24.1 1.4 %collective-permute-start.7 = (f32[160,256]{1,0:T(8,128)S(1)}, f32[160,256]{1,0:T(8,128)S(1)}, u32[]{:S(2)}, u32[]{:S(2)}) collective-permute-start(f32[160,256]{1,0:T(8,128)S(1)} %get-tuple-element.48), channel_id=1, source_target_pairs={{0,6},{1,7},{2,4},{3,5},{4,2},{5,3},{6,0},{7,1},{8,14},{9,15},{10,... | collective-permute-start | bytes 491528 | tf_op jit(solution)/shard_map/ppermute | solution.py:359
  25.7 2.0 %collective-permute-start.10 = (f32[136,256]{1,0:T(8,128)S(1)}, f32[136,256]{1,0:T(8,128)S(1)}, u32[]{:S(2)}, u32[]{:S(2)}) collective-permute-start(f32[136,256]{1,0:T(8,128)S(1)} %get-tuple-element.53), channel_id=1, source_target_pairs={{0,8},{1,9},{2,10},{3,11},{4,12},{5,13},{6,14},{7,15},{8,0},{9,1},... | collective-permute-start | bytes 417800 | tf_op jit(solution)/shard_map/ppermute | solution.py:359
  27.7 3.1 %collective-permute-done.10.refs_5_ = f32[136,256]{1,0:T(8,128)S(1)} collective-permute-done((f32[136,256]{1,0:T(8,128)S(1)}, f32[136,256]{1,0:T(8,128)S(1)}, u32[]{:S(2)}, u32[]{:S(2)}) %collective-permute-start.10) | collective-permute-done | bytes 139296 | tf_op jit(solution)/shard_map/ppermute | solution.py:359
  30.8 1.3 %collective-permute-done.6.refs_2_ = f32[160,256]{1,0:T(8,128)S(1)} collective-permute-done((f32[160,256]{1,0:T(8,128)S(1)}, f32[160,256]{1,0:T(8,128)S(1)}, u32[]{:S(2)}, u32[]{:S(2)}) %collective-permute-start.6) | collective-permute-done | bytes 163872 | tf_op jit(solution)/shard_map/ppermute | solution.py:359
  32.1 1.3 %collective-permute-done.5.refs_1_ = f32[160,256]{1,0:T(8,128)S(1)} collective-permute-done((f32[160,256]{1,0:T(8,128)S(1)}, f32[160,256]{1,0:T(8,128)S(1)}, u32[]{:S(2)}, u32[]{:S(2)}) %collective-permute-start.5) | collective-permute-done | bytes 163872 | tf_op jit(solution)/shard_map/ppermute | solution.py:359
  33.4 1.9 %shard_map.89 = (f32[128,256]{1,0:T(8,128)S(1)}, f32[160,256]{1,0:T(8,128)S(1)}, f32[4,128,256]{2,1,0:T(8,128)S(1)}, f32[2,136,256]{2,1,0:T(8,128)S(1)}) custom-call(s32[1]{0:T(128)} %bitcast.me_ref, f32[160,256]{1,0:T(8,128)S(1)} %get-tuple-element.45.refs_0_, f32[160,256]{1,0:T(8,128)S(1)} %collective-permute-done.5.refs_1_, ...), custom_call_target="tpu_custom_call" | custom-call | flops 452984832 | tf_op jit(solution)/shard_map/pallas_call | solution.py:371
  35.3 1.8 %collective-permute-start.9 = (f32[160,256]{1,0:T(8,128)S(1)}, f32[160,256]{1,0:T(8,128)S(1)}, u32[]{:S(2)}, u32[]{:S(2)}) collective-permute-start(f32[160,256]{1,0:T(8,128)S(1)} %get-tuple-element.51.refs_2_), channel_id=1, source_target_pairs={{0,8},{1,9},{2,10},{3,11},{4,12},{5,13},{6,14},{7,15},{8,0},{9,1},... | collective-permute-start | bytes 491528 | tf_op jit(solution)/shard_map/ppermute | solution.py:359
  37.1 2.6 %collective-permute-start.13 = (f32[136,256]{1,0:T(8,128)S(1)}, f32[136,256]{1,0:T(8,128)S(1)}, u32[]{:S(2)}, u32[]{:S(2)}) collective-permute-start(f32[136,256]{1,0:T(8,128)S(1)} %broadcast_select_fusion), channel_id=1, source_target_pairs={{0,16},{1,17},{2,18},{3,19},{4,20},{5,21},{6,22},{7,23},{8,24},{9,... | collective-permute-start | bytes 417800 | tf_op jit(solution)/shard_map/ppermute | solution.py:359
  39.8 3.1 %collective-permute-done.9.refs_3_ = f32[160,256]{1,0:T(8,128)S(1)} collective-permute-done((f32[160,256]{1,0:T(8,128)S(1)}, f32[160,256]{1,0:T(8,128)S(1)}, u32[]{:S(2)}, u32[]{:S(2)}) %collective-permute-start.9) | collective-permute-done | bytes 163872 | tf_op jit(solution)/shard_map/ppermute | solution.py:359
  43.5 2.0 %collective-permute-start.12 = (f32[160,256]{1,0:T(8,128)S(1)}, f32[160,256]{1,0:T(8,128)S(1)}, u32[]{:S(2)}, u32[]{:S(2)}) collective-permute-start(f32[160,256]{1,0:T(8,128)S(1)} %get-tuple-element.57.refs_2_), channel_id=1, source_target_pairs={{0,16},{1,17},{2,18},{3,19},{4,20},{5,21},{6,22},{7,23},{8,24},{9,... | collective-permute-start | bytes 491528 | tf_op jit(solution)/shard_map/ppermute | solution.py:359
  45.5 1.4 %collective-permute-done.14.refs_6_ = f32[136,256]{1,0:T(8,128)S(1)} collective-permute-done((f32[136,256]{1,0:T(8,128)S(1)}, f32[136,256]{1,0:T(8,128)S(1)}, u32[]{:S(2)}, u32[]{:S(2)}) %collective-permute-start.14) | collective-permute-done | bytes 139296 | tf_op jit(solution)/shard_map/ppermute | solution.py:359
  46.8 5.9 %collective-permute-done.12.refs_3_ = f32[160,256]{1,0:T(8,128)S(1)} collective-permute-done((f32[160,256]{1,0:T(8,128)S(1)}, f32[160,256]{1,0:T(8,128)S(1)}, u32[]{:S(2)}, u32[]{:S(2)}) %collective-permute-start.12) | collective-permute-done | bytes 163872 | tf_op jit(solution)/shard_map/ppermute | solution.py:359
  53.4 1.5 %collective-permute-start.15 = (f32[192,256]{1,0:T(8,128)S(1)}, f32[192,256]{1,0:T(8,128)S(1)}, u32[]{:S(2)}, u32[]{:S(2)}) collective-permute-start(f32[192,256]{1,0:T(8,128)S(1)} %get-tuple-element.62), channel_id=1, source_target_pairs={{0,2},{1,3},{2,0},{3,1},{4,6},{5,7},{6,4},{7,5},{8,10},{9,11},{10,... | collective-permute-start | bytes 589832 | tf_op jit(solution)/shard_map/ppermute | solution.py:359
  55.0 1.5 %collective-permute-start.16 = (f32[192,256]{1,0:T(8,128)S(1)}, f32[192,256]{1,0:T(8,128)S(1)}, u32[]{:S(2)}, u32[]{:S(2)}) collective-permute-start(f32[192,256]{1,0:T(8,128)S(1)} %get-tuple-element.63), channel_id=1, source_target_pairs={{0,4},{1,5},{2,6},{3,7},{4,0},{5,1},{6,2},{7,3},{8,12},{9,13},{10,... | collective-permute-start | bytes 589832 | tf_op jit(solution)/shard_map/ppermute | solution.py:359
  57.0 4.3 %collective-permute-done.15.refs_1_ = f32[192,256]{1,0:T(8,128)S(1)} collective-permute-done((f32[192,256]{1,0:T(8,128)S(1)}, f32[192,256]{1,0:T(8,128)S(1)}, u32[]{:S(2)}, u32[]{:S(2)}) %collective-permute-start.15) | collective-permute-done | bytes 196640 | tf_op jit(solution)/shard_map/ppermute | solution.py:359
  61.3 3.6 %collective-permute-done.16.refs_2_ = f32[192,256]{1,0:T(8,128)S(1)} collective-permute-done((f32[192,256]{1,0:T(8,128)S(1)}, f32[192,256]{1,0:T(8,128)S(1)}, u32[]{:S(2)}, u32[]{:S(2)}) %collective-permute-start.16) | collective-permute-done | bytes 196640 | tf_op jit(solution)/shard_map/ppermute | solution.py:359
  65.1 2.3 %collective-permute-done.18.refs_8_ = f32[4,192,256]{2,1,0:T(8,128)S(1)} collective-permute-done((f32[4,192,256]{2,1,0:T(8,128)S(1)}, f32[4,192,256]{2,1,0:T(8,128)S(1)}, u32[]{:S(2)}, u32[]{:S(2)}) %collective-permute-start.18) | collective-permute-done | bytes 786464 | tf_op jit(solution)/shard_map/ppermute | solution.py:359
  67.3 2.4 %shard_map.93 = (f32[512,1024]{1,0:T(8,128)}, f32[512,256]{1,0:T(8,128)}, f32[256,256]{1,0:T(8,128)}) custom-call(s32[1]{0:T(128)} %bitcast.me_ref, f32[192,256]{1,0:T(8,128)S(1)} %get-tuple-element.61.refs_0_, f32[192,256]{1,0:T(8,128)S(1)} %collective-permute-done.15.refs_1_, ...), custom_call_target="tpu_custom_call", output_to_operand_aliasing={{0}: (11, {}), {1}: (12, {})} | custom-call | tf_op jit(solution)/shard_map/pallas_call | solution.py:468
  (31 shorter events, 6.6 us)
Async XLA Ops:
  2.5 1.9 %collective-permute-start = (f32[2,136,256]{2,1,0:T(8,128)}, f32[2,136,256]{2,1,0:T(8,128)S(1)}, u32[]{:S(2)}, u32[]{:S(2)}) collective-permute-start(f32[2,136,256]{2,1,0:T(8,128)} %shard_map.85.packed_ref.refs_4_), channel_id=1, source_target_pairs={{0,1},{1,0},{2,3},{3,2},{4,5},{5,4},{6,7},{7,6},{8,9},{9,8},{10,11... | collective-permute-start | bytes 835592 | tf_op jit(solution)/shard_map/ppermute | solution.py:359
  5.4 13.1 %collective-permute-start.3 = (f32[136,256]{1,0:T(8,128)S(1)}, f32[136,256]{1,0:T(8,128)S(1)}, u32[]{:S(2)}, u32[]{:S(2)}) collective-permute-start(f32[136,256]{1,0:T(8,128)S(1)} %fusion.refs_0_), channel_id=1, source_target_pairs={{0,6},{1,7},{2,4},{3,5},{4,2},{5,3},{6,0},{7,1},{8,14},{9,15},{10,... | collective-permute-start | bytes 417800 | tf_op jit(solution)/shard_map/ppermute | solution.py:359
  9.3 9.2 %collective-permute-start.2 = (f32[136,256]{1,0:T(8,128)S(1)}, f32[136,256]{1,0:T(8,128)S(1)}, u32[]{:S(2)}, u32[]{:S(2)}) collective-permute-start(f32[136,256]{1,0:T(8,128)S(1)} %fusion.refs_0_), channel_id=1, source_target_pairs={{0,4},{1,5},{2,6},{3,7},{4,0},{5,1},{6,2},{7,3},{8,12},{9,13},{10,... | collective-permute-start | bytes 417800 | tf_op jit(solution)/shard_map/ppermute | solution.py:359
  9.8 8.7 %collective-permute-start.1 = (f32[136,256]{1,0:T(8,128)S(1)}, f32[136,256]{1,0:T(8,128)S(1)}, u32[]{:S(2)}, u32[]{:S(2)}) collective-permute-start(f32[136,256]{1,0:T(8,128)S(1)} %fusion.refs_0_), channel_id=1, source_target_pairs={{0,2},{1,3},{2,0},{3,1},{4,6},{5,7},{6,4},{7,5},{8,10},{9,11},{10,... | collective-permute-start | bytes 417800 | tf_op jit(solution)/shard_map/ppermute | solution.py:359
  9.9 11.0 %copy-start = (f32[2,136,256]{2,1,0:T(8,128)S(1)}, f32[2,136,256]{2,1,0:T(8,128)}, u32[]{:S(2)}) copy-start(f32[2,136,256]{2,1,0:T(8,128)} %shard_map.85.packed_ref.refs_4_) | copy-start | bytes 835588
  18.5 2.4 %collective-permute-start.4 = (f32[640,256]{1,0:T(8,128)}, f32[640,256]{1,0:T(8,128)S(1)}, u32[]{:S(2)}, u32[]{:S(2)}) collective-permute-start(f32[640,256]{1,0:T(8,128)} %get-tuple-element.44), channel_id=1, source_target_pairs={{0,1},{1,0},{2,3},{3,2},{4,5},{5,4},{6,7},{7,6},{8,9},{9,8},{10,11... | collective-permute-start | bytes 1966088 | tf_op jit(solution)/shard_map/ppermute | solution.py:359
  18.6 1.1 %copy-start.1 = (f32[640,256]{1,0:T(8,128)S(1)}, f32[640,256]{1,0:T(8,128)}, u32[]{:S(2)}) copy-start(f32[640,256]{1,0:T(8,128)} %get-tuple-element.38.refs_4_) | copy-start | bytes 1966084
  19.9 10.9 %collective-permute-start.8 = (f32[3,136,256]{2,1,0:T(8,128)S(1)}, f32[3,136,256]{2,1,0:T(8,128)S(1)}, u32[]{:S(2)}, u32[]{:S(2)}) collective-permute-start(f32[3,136,256]{2,1,0:T(8,128)S(1)} %get-tuple-element.49.refs_6_), channel_id=1, source_target_pairs={{0,1},{1,0},{2,3},{3,2},{4,5},{5,4},{6,7},{7,6},{8,9},{9,8},{10,11... | collective-permute-start | bytes 1253384 | tf_op jit(solution)/shard_map/ppermute | solution.py:359
  22.1 10.0 %collective-permute-start.6 = (f32[160,256]{1,0:T(8,128)S(1)}, f32[160,256]{1,0:T(8,128)S(1)}, u32[]{:S(2)}, u32[]{:S(2)}) collective-permute-start(f32[160,256]{1,0:T(8,128)S(1)} %get-tuple-element.47), channel_id=1, source_target_pairs={{0,4},{1,5},{2,6},{3,7},{4,0},{5,1},{6,2},{7,3},{8,12},{9,13},{10,... | collective-permute-start | bytes 491528 | tf_op jit(solution)/shard_map/ppermute | solution.py:359
  24.1 8.0 %collective-permute-start.7 = (f32[160,256]{1,0:T(8,128)S(1)}, f32[160,256]{1,0:T(8,128)S(1)}, u32[]{:S(2)}, u32[]{:S(2)}) collective-permute-start(f32[160,256]{1,0:T(8,128)S(1)} %get-tuple-element.48), channel_id=1, source_target_pairs={{0,6},{1,7},{2,4},{3,5},{4,2},{5,3},{6,0},{7,1},{8,14},{9,15},{10,... | collective-permute-start | bytes 491528 | tf_op jit(solution)/shard_map/ppermute | solution.py:359
  25.5 7.9 %collective-permute-start.5 = (f32[160,256]{1,0:T(8,128)S(1)}, f32[160,256]{1,0:T(8,128)S(1)}, u32[]{:S(2)}, u32[]{:S(2)}) collective-permute-start(f32[160,256]{1,0:T(8,128)S(1)} %get-tuple-element.46), channel_id=1, source_target_pairs={{0,2},{1,3},{2,0},{3,1},{4,6},{5,7},{6,4},{7,5},{8,10},{9,11},{10,... | collective-permute-start | bytes 491528 | tf_op jit(solution)/shard_map/ppermute | solution.py:359
  25.7 5.1 %collective-permute-start.10 = (f32[136,256]{1,0:T(8,128)S(1)}, f32[136,256]{1,0:T(8,128)S(1)}, u32[]{:S(2)}, u32[]{:S(2)}) collective-permute-start(f32[136,256]{1,0:T(8,128)S(1)} %get-tuple-element.53), channel_id=1, source_target_pairs={{0,8},{1,9},{2,10},{3,11},{4,12},{5,13},{6,14},{7,15},{8,0},{9,1},... | collective-permute-start | bytes 417800 | tf_op jit(solution)/shard_map/ppermute | solution.py:359
  30.8 9.0 %collective-permute-start.11 = (f32[136,256]{1,0:T(8,128)S(1)}, f32[136,256]{1,0:T(8,128)S(1)}, u32[]{:S(2)}, u32[]{:S(2)}) collective-permute-start(f32[136,256]{1,0:T(8,128)S(1)} %collective-permute-done.10.refs_5_), channel_id=1, source_target_pairs={{0,1},{1,0},{2,3},{3,2},{4,5},{5,4},{6,7},{7,6},{8,9},{9,8},{10,11... | collective-permute-start | bytes 417800 | tf_op jit(solution)/shard_map/ppermute | solution.py:359
  35.3 7.5 %collective-permute-start.9 = (f32[160,256]{1,0:T(8,128)S(1)}, f32[160,256]{1,0:T(8,128)S(1)}, u32[]{:S(2)}, u32[]{:S(2)}) collective-permute-start(f32[160,256]{1,0:T(8,128)S(1)} %get-tuple-element.51.refs_2_), channel_id=1, source_target_pairs={{0,8},{1,9},{2,10},{3,11},{4,12},{5,13},{6,14},{7,15},{8,0},{9,1},... | collective-permute-start | bytes 491528 | tf_op jit(solution)/shard_map/ppermute | solution.py:359
  37.1 8.3 %collective-permute-start.13 = (f32[136,256]{1,0:T(8,128)S(1)}, f32[136,256]{1,0:T(8,128)S(1)}, u32[]{:S(2)}, u32[]{:S(2)}) collective-permute-start(f32[136,256]{1,0:T(8,128)S(1)} %broadcast_select_fusion), channel_id=1, source_target_pairs={{0,16},{1,17},{2,18},{3,19},{4,20},{5,21},{6,22},{7,23},{8,24},{9,... | collective-permute-start | bytes 417800 | tf_op jit(solution)/shard_map/ppermute | solution.py:359
  43.5 23.9 %copy-start.2 = (f32[256,256]{1,0:T(8,128)S(1)}, f32[256,256]{1,0:T(8,128)}, u32[]{:S(2)}) copy-start(f32[256,256]{1,0:T(8,128)} %refs_9_.1) | copy-start | bytes 786436
  43.5 9.2 %collective-permute-start.12 = (f32[160,256]{1,0:T(8,128)S(1)}, f32[160,256]{1,0:T(8,128)S(1)}, u32[]{:S(2)}, u32[]{:S(2)}) collective-permute-start(f32[160,256]{1,0:T(8,128)S(1)} %get-tuple-element.57.refs_2_), channel_id=1, source_target_pairs={{0,16},{1,17},{2,18},{3,19},{4,20},{5,21},{6,22},{7,23},{8,24},{9,... | collective-permute-start | bytes 491528 | tf_op jit(solution)/shard_map/ppermute | solution.py:359
  45.5 1.4 %collective-permute-start.14 = (f32[136,256]{1,0:T(8,128)S(1)}, f32[136,256]{1,0:T(8,128)S(1)}, u32[]{:S(2)}, u32[]{:S(2)}) collective-permute-start(f32[136,256]{1,0:T(8,128)S(1)} %collective-permute-done.13.refs_5_), channel_id=1, source_target_pairs={{0,1},{1,0},{2,3},{3,2},{4,5},{5,4},{6,7},{7,6},{8,9},{9,8},{10,11... | collective-permute-start | bytes 417800 | tf_op jit(solution)/shard_map/ppermute | solution.py:359
  53.4 7.9 %collective-permute-start.15 = (f32[192,256]{1,0:T(8,128)S(1)}, f32[192,256]{1,0:T(8,128)S(1)}, u32[]{:S(2)}, u32[]{:S(2)}) collective-permute-start(f32[192,256]{1,0:T(8,128)S(1)} %get-tuple-element.62), channel_id=1, source_target_pairs={{0,2},{1,3},{2,0},{3,1},{4,6},{5,7},{6,4},{7,5},{8,10},{9,11},{10,... | collective-permute-start | bytes 589832 | tf_op jit(solution)/shard_map/ppermute | solution.py:359
  55.0 9.9 %collective-permute-start.16 = (f32[192,256]{1,0:T(8,128)S(1)}, f32[192,256]{1,0:T(8,128)S(1)}, u32[]{:S(2)}, u32[]{:S(2)}) collective-permute-start(f32[192,256]{1,0:T(8,128)S(1)} %get-tuple-element.63), channel_id=1, source_target_pairs={{0,4},{1,5},{2,6},{3,7},{4,0},{5,1},{6,2},{7,3},{8,12},{9,13},{10,... | collective-permute-start | bytes 589832 | tf_op jit(solution)/shard_map/ppermute | solution.py:359
  56.5 8.4 %collective-permute-start.17 = (f32[192,256]{1,0:T(8,128)S(1)}, f32[192,256]{1,0:T(8,128)S(1)}, u32[]{:S(2)}, u32[]{:S(2)}) collective-permute-start(f32[192,256]{1,0:T(8,128)S(1)} %get-tuple-element.64), channel_id=1, source_target_pairs={{0,6},{1,7},{2,4},{3,5},{4,2},{5,3},{6,0},{7,1},{8,14},{9,15},{10,... | collective-permute-start | bytes 589832 | tf_op jit(solution)/shard_map/ppermute | solution.py:359
  65.0 2.4 %collective-permute-start.18 = (f32[4,192,256]{2,1,0:T(8,128)S(1)}, f32[4,192,256]{2,1,0:T(8,128)S(1)}, u32[]{:S(2)}, u32[]{:S(2)}) collective-permute-start(f32[4,192,256]{2,1,0:T(8,128)S(1)} %shard_map.92), channel_id=1, source_target_pairs={{0,1},{1,0},{2,3},{3,2},{4,5},{5,4},{6,7},{7,6},{8,9},{9,8},{10,11... | collective-permute-start | bytes 2359304 | tf_op jit(solution)/shard_map/ppermute | solution.py:359
